TPU v7x, 128 devices: a whole 4x4x4 slice. The times are simulated.
128 devices in a mesh: row: 16 (over z_hi, y, core), col: 8 (over x, z_lo).
Axes of the slice: x: 4, y: 4, z: 4 (z_hi: 2, z_lo: 2; z = z_hi * 2 + z_lo), core: 2. Of those that a mesh axis runs over, the one named last changes fastest.
Arguments:
- matrix: bfloat16 [8192, 8192], P('row'), as said below
- position: int32 [128], replicated, may hold values from 0 to 127, as said below
- square_pattern: int32 [128, 128], replicated, may hold values from 0 to 1, as said below
- iterate_pattern: int32 [128, 128], replicated, may hold values from 0 to 1, as said below
Outputs:
- square: bfloat16 [8192, 8192], P('row', 'col')
- iterate: bfloat16 [8192, 8192], P('row', 'col')
Inputs may be any that keep to these rules, and one draw needn't show every extreme that they name: matrix is exactly symmetric. A permutation; the 8 blocks b that share b // 8 have distinct values of position // 8. `square_pattern`: symmetric, ones on the diagonal. `iterate_pattern`: symmetric, ones on the diagonal.
All inputs are finite; a program needn't handle non-finite values.
Results may differ from a plain program's by a relative error of at most 0.0043.
Values may be sent and summed in bfloat16 or wider, within the bound.
A program may use at most 128 MiB of HBM per device.

v0:
```python
import jax
import jax.numpy as jnp
from jax import lax
from jax.sharding import PartitionSpec as P

BW = 64


def per_device(matrix, position, square_pattern, iterate_pattern):
    rows_here = matrix.shape[0]
    columns_all = matrix.shape[1]
    blocks = columns_all // BW
    row_blocks = rows_here // BW
    grid_rows = lax.axis_size("row")
    grid_cols = lax.axis_size("col")
    col_blocks = blocks // grid_cols
    row_index = lax.axis_index("row")
    col_index = lax.axis_index("col")
    numbers = jnp.arange(blocks, dtype=jnp.int32)
    inverse = jnp.sum(jnp.where(position[:, None] == numbers[None, :], numbers[:, None], 0), axis=0)
    col_atoms = lax.dynamic_slice_in_dim(inverse, col_index * col_blocks, col_blocks)
    row_atoms = lax.dynamic_slice_in_dim(inverse, row_index * row_blocks, row_blocks)
    stripe = jnp.take(matrix.reshape(rows_here, blocks, BW), col_atoms, axis=1).reshape(
        rows_here, col_blocks * BW
    )
    my_targets = (
        lax.dynamic_slice_in_dim(position, row_index * row_blocks, row_blocks) // row_blocks
    )
    targets = jnp.arange(grid_rows, dtype=jnp.int32)
    choose = (targets[:, None] == my_targets[None, :]).astype(jnp.bfloat16)
    outgoing = jnp.einsum(
        "ta,abc->tbc",
        choose,
        stripe.reshape(row_blocks, BW, col_blocks * BW),
        preferred_element_type=jnp.float32,
    ).astype(jnp.bfloat16)
    arrived = lax.all_to_all(outgoing, "row", split_axis=0, concat_axis=0, tiled=True)
    sources = row_atoms // row_blocks
    selector = (sources[:, None] == targets[None, :]).astype(jnp.bfloat16)
    own_block = (
        jnp.einsum("ys,sbc->ybc", selector, arrived, preferred_element_type=jnp.float32)
        .astype(jnp.bfloat16)
        .reshape(rows_here, col_blocks * BW)
    )
    first_columns = lax.all_gather(own_block, "row", axis=0, tiled=True)
    square_mask = jnp.take(jnp.take(square_pattern, row_atoms, axis=0), col_atoms, axis=1).astype(
        jnp.float32
    )
    iterate_mask = jnp.take(jnp.take(iterate_pattern, row_atoms, axis=0), col_atoms, axis=1).astype(
        jnp.float32
    )

    def multiply(columns):
        return jnp.dot(
            lax.all_gather(own_block, "col", axis=1, tiled=True),
            columns,
            preferred_element_type=jnp.float32,
        )

    def filtered(values, filter_mask):
        shaped = values.reshape(row_blocks, BW, col_blocks, BW) * filter_mask[:, None, :, None]
        return shaped.reshape(rows_here, col_blocks * BW)

    square = filtered(multiply(first_columns), square_mask).astype(jnp.bfloat16)
    second_columns = lax.all_gather(square, "row", axis=0, tiled=True)
    product = multiply(second_columns)
    iterate = filtered(0.5 * (3.0 * own_block.astype(jnp.float32) - product), iterate_mask).astype(
        jnp.bfloat16
    )
    return (square, iterate)


def solution(mesh):
    return jax.shard_map(
        per_device,
        mesh=mesh,
        in_specs=(P("row", None), P(), P(), P()),
        out_specs=(P("row", "col"), P("row", "col")),
        check_vma=False,
    )
```

profile of v0, /device:TPU:1, one launch (start us, length us, event | category | flops | bytes accessed | tf_op | source)
XLA Modules:
  0.0 504.1 jit_solution(9198660955971613281)
XLA Ops:
  7.2 0.8 select_reduce_fusion
  8.1 12.0 %copy.37 = bf16[512,8192]{0,1:T(8,128)(2,1)} copy(bf16[512,8192]{1,0:T(8,128)(2,1)} %param.8) | data formatting | bytes 16777216 | tf_op args[0]
  20.1 4.0 gather_fusion
  24.1 1.1 reshape.95
  25.2 1.4 copy.47
  26.7 0.1 broadcast_in_dim.58
  26.9 0.1 broadcast_select_fusion
  27.0 0.9 convolution_convert_fusion
  27.9 2.5 copy.40
  30.4 9.3 %all-to-all-start = ((bf16[16,64,1024]{2,1,0:T(8,128)(2,1)}), bf16[16,64,1024]{2,1,0:T(8,128)(2,1)S(1)}, u32[]{:S(2)}, u32[]{:S(2)}) async-start(bf16[16,64,1024]{2,1,0:T(8,128)(2,1)} %copy.40), calls=%async_computation | async-start | bytes 4194304 | tf_op jit(solution)/shard_map/all_to_all | solution.py:37
  39.8 0.1 and_select_fusion.1
  39.8 28.5 %all-to-all-done = bf16[16,64,1024]{2,1,0:T(8,128)(2,1)S(1)} async-done(((bf16[16,64,1024]{2,1,0:T(8,128)(2,1)}), bf16[16,64,1024]{2,1,0:T(8,128)(2,1)S(1)}, u32[]{:S(2)}, u32[]{:S(2)}) %all-to-all-start) | async-done | bytes 2097184 | tf_op jit(solution)/shard_map/all_to_all | solution.py:37
  68.3 1.3 fusion.2
  69.6 1.5 copy.42
  71.2 0.7 all-gather.6.cloned.1.call-update
  71.9 0.2 all-gather.8.cloned.1.call-start
  72.1 0.1 compare_and_fusion
  72.2 0.6 gather_fusion.3
  72.8 0.6 gather_fusion.1
  73.4 0.1 copy.45
  73.5 0.6 gather_fusion.4
  74.2 0.1 copy.43
  74.3 0.6 gather_fusion.2
  74.9 2.3 mul.43
  77.2 3.6 mul.44
  80.9 158.3 %all-gather.4.cloned.1.call-done = bf16[512,8192]{1,0:T(8,128)(2,1)} async-done(((bf16[512,1024]{1,0:T(8,128)(2,1)}), bf16[512,8192]{1,0:T(8,128)(2,1)}) %all-gather.4.cloned.1.call-update) | async-done | bytes 8388624 | tf_op jit(solution)/shard_map/all_gather | solution.py:55
  239.1 119.2 %all-gather.6.cloned.1.call-done = bf16[8192,1024]{1,0:T(8,128)(2,1)} async-done(((bf16[512,1024]{1,0:T(8,128)(2,1)}), bf16[8192,1024]{1,0:T(8,128)(2,1)}) %all-gather.6.cloned.1.call-update) | async-done | bytes 16777232 | tf_op jit(solution)/shard_map/all_gather | solution.py:45
  358.3 15.6 %multiply_convert_fusion.1 = bf16[512,1024]{1,0:T(8,128)(2,1)} fusion(f32[512,1024]{1,0:T(8,128)S(1)} %mul.44, bf16[512,8192]{1,0:T(8,128)(2,1)} %all-gather.4.cloned.1.call-done, bf16[8192,1024]{1,0:T(8,128)(2,1)} %all-gather.6.cloned.1.call-done), kind=kOutput, calls=%fused_computation.8 | convolution fusion | flops 8590983168 | bytes 28311552 | tf_op jit(solution)/shard_map/dot_general | solution.py:54
  373.9 2.3 mul.50
  376.2 3.6 mul.51
  379.8 102.1 %all-gather.8.cloned.1.call-done = bf16[8192,1024]{1,0:T(8,128)(2,1)} async-done(((bf16[512,1024]{1,0:T(8,128)(2,1)}), bf16[8192,1024]{1,0:T(8,128)(2,1)}) %all-gather.8.cloned.1.call-update) | async-done | bytes 16777232 | tf_op jit(solution)/shard_map/all_gather | solution.py:65
  482.0 15.6 %multiply_convert_fusion = bf16[512,1024]{1,0:T(8,128)(2,1)} fusion(f32[512,1024]{1,0:T(8,128)S(1)} %mul.51, bf16[512,1024]{1,0:T(8,128)(2,1)S(1)} %bitcast.27, bf16[512,8192]{1,0:T(8,128)(2,1)} %all-gather.4.cloned.1.call-done, bf16[8192,1024]{1,0:T(8,128)(2,1)} %all-gather.8.cloned.1.call-done), kind=kOutput, calls=%fused_computation.7 | convolution fusion | flops 8593080320 | bytes 29360128 | tf_op jit(solution)/shard_map/dot_general | solution.py:54
  (23 shorter events, 0.6 us)
Async XLA Ops:
  7.2 65.1 %copy-start = (s32[128,128]{1,0:T(8,128)S(1)}, s32[128,128]{1,0:T(8,128)}, u32[]{:S(2)}) copy-start(s32[128,128]{1,0:T(8,128)} %param.11) | copy-start | bytes 196612
  25.2 1.6 copy-start.4
  30.4 37.9 %all-to-all-start = ((bf16[16,64,1024]{2,1,0:T(8,128)(2,1)}), bf16[16,64,1024]{2,1,0:T(8,128)(2,1)S(1)}, u32[]{:S(2)}, u32[]{:S(2)}) async-start(bf16[16,64,1024]{2,1,0:T(8,128)(2,1)} %copy.40), calls=%async_computation | async-start | bytes 4194304 | tf_op jit(solution)/shard_map/all_to_all | solution.py:37
  39.7 199.4 %all-gather.4.cloned.1.call-start = ((), (), s32[]{:S(2)}) async-start(), calls=%async_computation.1 | async-start | bytes 9437184 | tf_op jit(solution)/shard_map/all_gather | solution.py:55
  69.6 3.2 copy-start.3
  71.2 287.2 %all-gather.6.cloned.1.call-start = ((), (), s32[]{:S(2)}) async-start(), calls=%async_computation.2 | async-start | bytes 17825792 | tf_op jit(solution)/shard_map/all_gather | solution.py:45
  71.9 410.0 %all-gather.8.cloned.1.call-start = ((), (), s32[]{:S(2)}) async-start(), calls=%async_computation.3 | async-start | bytes 17825792 | tf_op jit(solution)/shard_map/all_gather | solution.py:65
  376.2 105.7 %copy-start.2 = (bf16[8,64,1024]{2,1,0:T(8,128)(2,1)S(1)}, bf16[8,64,1024]{2,1,0:T(8,128)(2,1)}, u32[]{:S(2)}) copy-start(bf16[8,64,1024]{2,1,0:T(8,128)(2,1)} %copy.42) | copy-start | bytes 3145732
  481.9 15.6 %copy-start.1 = (s32[128,128]{1,0:T(8,128)S(1)}, s32[128,128]{1,0:T(8,128)}, u32[]{:S(2)}) copy-start(s32[128,128]{1,0:T(8,128)} %param.11) | copy-start | bytes 196612
Sparse Core Ops, SparseCore 0:
  71.3 167.7 all-gather.3
  242.1 116.1 all-gather.5
  374.0 107.8 all-gather.7
where the time goes:
time: 505 us; the launch traced here: 504 us
  waiting for transfers between devices  409 us (81%)
  local copies, waits for them, and re-layouts  37.2 us (7%)
  matrix products  33.4 us (7%)
  between operations  13.9 us (3%)
  starting transfers between devices  9.6 us (2%)
    all_gather x1, waiting for transfers between devices, multiply(): lax.all_gather(own_block, 'col', axis=1, tiled=True)  158 us
    all_gather x1, waiting for transfers between devices, per_device(): first_columns = lax.all_gather(own_block, 'row', axis=0, tiled=True)  119 us
    all_gather x1, waiting for transfers between devices, per_device(): second_columns = lax.all_gather(square, 'row', axis=0, tiled=True)  102 us
    dot_general x2, matrix products, multiply(): jnp.dot(lax.all_gather(own_block, 'col', axis=1, tiled=True), columns, pr...  31.2 us
    all_to_all x1, waiting for transfers between devices, per_device(): lax.all_to_all(outgoing, 'row', split_axis=0, concat_axis=0, tiled=True)  28.5 us
    unnamed x11, local copies, waits for them, and re-layouts  12 us
    mul x4, local copies, waits for them, and re-layouts, filtered(): values.reshape(row_blocks, BW, col_blocks, BW)  11.8 us
  transfers between devices with their start and end apart: 4, of which 4 were waited for; matrix products, arithmetic and copies ran while one was open for 3% of the time, Pallas kernels for 0%

commit v1 on v0

v1 whole, which is shorter than its diff:
```python
import functools

import jax
import jax.numpy as jnp
from jax import lax
from jax.experimental import pallas as pl
from jax.experimental.pallas import tpu as pltpu
from jax.sharding import PartitionSpec as P

BW = 64
M = 8192
NB = M // BW
ROWS = 512
NR = 16
NC = 8
NCH = 4
CB = NR // NCH
CW = CB * BW
KT = NC * CW
SUB = 16
UNITS = ROWS // SUB
PARTS = ((0, 11), (11, 11), (22, 10))
MESH = pl.DeviceIdType.MESH
BF = jnp.bfloat16
F32 = jnp.float32


def flip(v, b):
    return v + b - 2 * v * b


def kernel(
    first, pair, source, slot, m_hbm, pos_row, sq_pat, it_pat,
    sq_ref, it_ref,
    mine, mg, fg, facc, slots_out, mgp, acc, tt, got1, got2, msq, mit, odd,
    xs, xr, ds, dr, as_, ar, ns, nr, t1s, t1r, t2s, t2r, loc, m_sem, *slots_in,
):
    r = lax.axis_index("row")
    c = lax.axis_index("col")
    k = r % 2
    y = (r // 2) % 4
    zh = r // 8
    x = c // 2
    zl = c % 2
    jz = flip(zl, zh)
    lab = x * 2 + jz

    def row_of(zh_, y_, k_):
        return (zh_ * 4 + y_) * 2 + k_

    def group_col(row):
        return x * 2 + flip(jz, row // 8)

    def outer(mask):
        y_ = y
        if mask & 1:
            y_ = y_ + 1 - 2 * (y_ % 2)
        if mask & 2:
            y_ = 3 - y_
        zh_ = 1 - zh if mask & 4 else zh
        return row_of(zh_, y_, k)

    def inner(mask):
        x_ = x
        if mask & 1:
            x_ = x_ + 1 - 2 * (x_ % 2)
        if mask & 2:
            x_ = 3 - x_
        zl_ = 1 - zl if mask & 4 else zl
        return x_, zl_

    def inner_lab(mask):
        x_, zl_ = inner(mask)
        return x_ * 2 + flip(zl_, zh)

    outer_dev = [(outer(1 << d), group_col(outer(1 << d))) for d in range(3)]
    inner_dev = [(r, inner(1 << d)[0] * 2 + inner(1 << d)[1]) for d in range(3)]
    sibling = (r + 1 - 2 * k, c)

    @pl.loop(0, NB // 2)
    def _(i):
        at = pl.ds(pl.multiple_of(i * 128, 128), 128)
        pltpu.make_async_copy(m_hbm.at[:, at], mine.at[i], m_sem).start()

    barrier = pltpu.get_barrier_semaphore()
    for d in range(1, NR):
        t = lax.rem(r + d, NR)
        pl.semaphore_signal(barrier, inc=1, device_id=(t, group_col(t)), device_id_type=MESH)
    for d in range(1, NC):
        pl.semaphore_signal(
            barrier, inc=1, device_id=(r, lax.rem(c + d, NC)), device_id_type=MESH
        )

    block_id = lax.broadcasted_iota(jnp.int32, (NR, NB), 0)
    cols_hot = (pos_row[...] == 8 * block_id + lab).astype(F32)
    row_id = lax.broadcasted_iota(jnp.int32, (8, NB), 0)
    rows_hot = (pos_row[...] == 8 * r + row_id).astype(F32)
    wide = (
        lax.broadcasted_iota(jnp.int32, (NR, NR * BW), 1) // BW
        == lax.broadcasted_iota(jnp.int32, (NR, NR * BW), 0)
    ).astype(F32)

    def columns_of(rows):
        small = lax.dot_general(
            rows, cols_hot, (((1,), (1,)), ((), ())), preferred_element_type=F32
        )
        return jnp.dot(small, wide, preferred_element_type=F32)

    parity = (lax.broadcasted_iota(jnp.int32, (8, NB), 1) % 2).astype(F32)
    odd[...] = columns_of(parity)
    msq[...] = columns_of(sq_pat[pl.ds(pl.multiple_of(8 * r, 8), 8), :].astype(F32))
    mit[...] = columns_of(
        jnp.dot(rows_hot, it_pat[...].astype(F32), preferred_element_type=F32)
    )

    lane = lax.broadcasted_iota(jnp.int32, (ROWS, 2 * BW), 1)
    pltpu.make_async_copy(mine, mine, m_sem).wait()
    for i in range(NR // 2):
        w0 = mine[pair[8 * (2 * i) + lab]].astype(F32)
        w1 = mine[pair[8 * (2 * i + 1) + lab]].astype(F32)
        o = odd[0:1, i * 128 : (i + 1) * 128]
        lo = w0 * (1.0 - o) + pltpu.roll(w0, BW, 1) * o
        hi = w1 * o + pltpu.roll(w1, BW, 1) * (1.0 - o)
        both = jnp.where(lane < BW, lo, hi).astype(BF).reshape(UNITS, SUB, 128)
        j, off = (2 * i) // CB, ((2 * i) % CB) * BW
        mg[j, pl.ds(r * UNITS, UNITS), :, off : off + 128] = both

    pl.semaphore_wait(barrier, NR + NC - 2)

    def subs(order, o):
        out = [0]
        for d in order[:o]:
            out += [s | (1 << d) for s in out]
        return out

    def outer_copy(j, p, sub, d):
        lo, n = PARTS[p]
        at = mg.at[j, pl.ds(outer(sub) * UNITS + lo, n)]
        mask = sub | (1 << d)
        return pltpu.make_async_remote_copy(
            src_ref=at, dst_ref=at, send_sem=xs.at[j, p, mask - 1], recv_sem=xr.at[j, p, mask - 1],
            device_id=outer_dev[d], device_id_type=MESH,
        )

    def outer_arrival(j, p, mask, d):
        lo, n = PARTS[p]
        at = mg.at[j, pl.ds(outer(mask) * UNITS + lo, n)]
        return pltpu.make_async_remote_copy(
            src_ref=at, dst_ref=at, send_sem=xs.at[j, p, mask - 1], recv_sem=xr.at[j, p, mask - 1],
            device_id=outer_dev[d], device_id_type=MESH,
        )

    def inner_copy(j, p, sub, d, m):
        lo, n = PARTS[p]
        at = fg.at[j, pl.ds(lo * SUB, n * SUB), pl.ds(pl.multiple_of(inner_lab(sub) * CW, CW), CW)]
        return pltpu.make_async_remote_copy(
            src_ref=at, dst_ref=at, send_sem=ns.at[j, p, m - 1], recv_sem=nr.at[j, p, m - 1],
            device_id=inner_dev[d], device_id_type=MESH,
        )

    def orders():
        for p in range(3):
            yield p, [(p + i) % 3 for i in range(3)]

    def outer_send(j, o):
        for sub_i in range(1 << o):
            for p, order in orders():
                outer_copy(j, p, subs(order, o)[sub_i], order[o]).start()

    def outer_wait(j, o):
        for p, order in orders():
            for sub in subs(order, o):
                outer_arrival(j, p, sub | (1 << order[o]), order[o]).wait_recv()

    def inner_send(j, o):
        for sub_i in range(1 << o):
            for p, order in orders():
                sub = subs(order, o)[sub_i]
                inner_copy(j, p, sub, order[o], sub | (1 << order[o])).start()

    def inner_wait(j, o):
        for p, order in orders():
            for sub in subs(order, o):
                m = sub | (1 << order[o])
                inner_copy(j, p, m, order[o], m).wait_recv()

    def sib_copy(j, m, mine=True):
        row = outer(m)
        if not mine:
            row = row + 1 - 2 * k
        at = mg.at[j, pl.ds(row * UNITS, UNITS)]
        return pltpu.make_async_remote_copy(
            src_ref=at, dst_ref=at, send_sem=ds.at[j, m], recv_sem=dr.at[j, m],
            device_id=sibling, device_id_type=MESH,
        )

    def a2a_copy(j, t, src_row):
        return pltpu.make_async_remote_copy(
            src_ref=slots_out.at[j, t], dst_ref=slots_in[j].at[src_row],
            send_sem=as_.at[j, t], recv_sem=ar.at[j, src_row],
            device_id=(t, group_col(t)), device_id_type=MESH,
        )

    def a2a_local(j):
        return pltpu.make_async_copy(slots_out.at[j, r], slots_in[j].at[r], loc.at[j])

    def first_product(j):
        facc[...] = jnp.zeros_like(facc)

        @pl.loop(0, 8)
        def _(kt):
            left = jnp.concatenate([mine[kt * 8 + i] for i in range(8)], axis=1)
            right = mg[j, pl.ds(kt * 64, 64)].reshape(1024, CW)
            prod = jnp.dot(left, right, preferred_element_type=F32)
            facc[...] += prod.reshape(8, BW, CW)

        for a in range(8):
            facc[a] = facc[a] * msq[a : a + 1, j * CW : (j + 1) * CW]
        for t in range(NR):
            slots_out[j, t] = facc[slot[NR * r + t]].astype(BF)

    def a2a_send(j):
        for d in range(1, NR):
            a2a_copy(j, lax.rem(r + d, NR), r).start()
        a2a_local(j).start()

    def a2a_wait(j):
        for d in range(1, NR):
            t = lax.rem(r + NR - d, NR)
            a2a_copy(j, t, t).wait_recv()
        a2a_local(j).wait()

    def take_rows(j):
        for p in range(8):
            fg[j, p * BW : (p + 1) * BW, pl.ds(pl.multiple_of(lab * CW, CW), CW)] = slots_in[j][
                source[8 * r + p]
            ]

    def second_product(j):
        @pl.loop(0, NC)
        def _(n):
            for i in range(CB):
                src = first[8 * (j * CB + i) + n]
                for u in range(BW // SUB):
                    at = pl.ds(pl.multiple_of(n * CW + i * BW + u * SUB, SUB), SUB)
                    for jj in range(NCH):
                        mgp[at, jj * CW : (jj + 1) * CW] = mg[jj, src + u]

        @pl.loop(0, M // NC // 256)
        def _(nt):
            at = pl.ds(pl.multiple_of(nt * 256, 256), 256)
            prod = jnp.dot(fg[j], mgp[:, at], preferred_element_type=F32)
            if j == 0:
                acc[:, at] = prod
            else:
                acc[:, at] += prod

    def last_piece(jj):
        for p in range(8):
            src = first[8 * r + p]
            for u in range(BW // SUB):
                own = mg[jj, src + u].astype(F32)
                lo = p * BW + u * SUB
                at = (slice(lo, lo + SUB), slice(jj * CW, (jj + 1) * CW))
                acc[at] = (0.5 * (3.0 * own - acc[at])) * mit[p : p + 1, jj * CW : (jj + 1) * CW]
        turned = acc[:, jj * CW : (jj + 1) * CW].T.astype(BF)
        for i in range(CB):
            tt[jj * CB + i] = turned[i * BW : (i + 1) * BW, :]

    def turn1(t, src_row):
        return pltpu.make_async_remote_copy(
            src_ref=tt.at[t], dst_ref=got1.at[src_row], send_sem=t1s.at[t], recv_sem=t1r.at[src_row],
            device_id=(t, group_col(t)), device_id_type=MESH,
        )

    def turn2(col, src_lab):
        return pltpu.make_async_remote_copy(
            src_ref=got1.at[pl.ds(2 * col, 2)], dst_ref=got2.at[src_lab],
            send_sem=t2s.at[col], recv_sem=t2r.at[src_lab],
            device_id=(r, col), device_id_type=MESH,
        )

    def square_out():
        jc = c // (NC // NCH)
        i0 = (2 * c) % CB
        for h in range(4):
            w = [
                fg[jc, :, pl.ds(pl.multiple_of(n * CW + i0 * BW, 128), 128)].astype(F32)
                for n in (2 * h, 2 * h + 1)
            ]
            sq_ref[:, h * 128 : (h + 1) * 128] = jnp.where(
                lane < BW, w[0], pltpu.roll(w[1], BW, 1)
            ).astype(BF)
            sq_ref[:, 512 + h * 128 : 512 + (h + 1) * 128] = jnp.where(
                lane < BW, pltpu.roll(w[0], BW, 1), w[1]
            ).astype(BF)

    def when(j, f, *args):
        if 0 <= j < NCH:
            f(j, *args)

    for i in range(NCH + 8):
        when(i, outer_send, 0)
        if 0 <= i - 1 < NCH:
            outer_wait(i - 1, 0)
            outer_send(i - 1, 1)
        if 0 <= i - 2 < NCH:
            outer_wait(i - 2, 1)
            outer_send(i - 2, 2)
        if 0 <= i - 3 < NCH:
            outer_wait(i - 3, 2)
            for m in range(8):
                sib_copy(i - 3, m).start()
        if 0 <= i - 5 < NCH:
            a2a_wait(i - 5)
            take_rows(i - 5)
            inner_send(i - 5, 0)
        if 0 <= i - 6 < NCH:
            inner_wait(i - 6, 0)
            inner_send(i - 6, 1)
        if 0 <= i - 7 < NCH:
            inner_wait(i - 7, 1)
            inner_send(i - 7, 2)
        if 0 <= i - 4 < NCH:
            for m in range(8):
                sib_copy(i - 4, m, mine=False).wait_recv()
            first_product(i - 4)
            a2a_send(i - 4)
        if 0 <= i - 8 < NCH:
            inner_wait(i - 8, 2)
            second_product(i - 8)

    for jj in range(NCH):
        last_piece(jj)
        for i in range(CB):
            t = jj * CB + i

            @pl.when(t != r)
            def _():
                turn1(t, r).start()

            @pl.when(t == r)
            def _():
                pltpu.make_async_copy(tt.at[t], got1.at[t], loc.at[NCH]).start()

    square_out()
    for d in range(1, NR):
        t = lax.rem(r + NR - d, NR)
        turn1(t, t).wait_recv()
    pltpu.make_async_copy(tt.at[r], got1.at[r], loc.at[NCH]).wait()
    for d in range(1, NC):
        turn2(lax.rem(c + d, NC), lab).start()
    here = pltpu.make_async_copy(got1.at[pl.ds(2 * c, 2)], got2.at[lab], loc.at[NCH + 1])
    here.start()
    for n in range(1, NC):
        col = lax.rem(c + NC - n, NC)
        src = 2 * (col // 2) + flip(col % 2, zh)
        turn2(col, src).wait_recv()
    here.wait()
    for n in range(NC):
        for h in range(2):
            it_ref[n * BW : (n + 1) * BW, h * ROWS : (h + 1) * ROWS] = got2[n, h]

    for j in range(NCH):
        for o in range(3):
            for p, order in orders():
                for sub in subs(order, o):
                    outer_copy(j, p, sub, order[o]).wait_send()
                    inner_copy(j, p, sub, order[o], sub | (1 << order[o])).wait_send()
        for m in range(8):
            sib_copy(j, m).wait_send()
        for d in range(1, NR):
            a2a_copy(j, lax.rem(r + d, NR), r).wait_send()
    for d in range(1, NR):
        turn1(lax.rem(r + d, NR), r).wait_send()
    for d in range(1, NC):
        turn2(lax.rem(c + d, NC), lab).wait_send()


def per_device(matrix, position, square_pattern, iterate_pattern):
    numbers = jnp.arange(NB, dtype=jnp.int32)
    inverse = jnp.sum(jnp.where(position[:, None] == numbers[None, :], numbers[:, None], 0), axis=0)
    target = position.reshape(NR, 1, 8) // 8
    hits = target == jnp.arange(NR, dtype=jnp.int32)[None, :, None]
    slot = jnp.sum(jnp.where(hits, jnp.arange(8, dtype=jnp.int32), 0), axis=2)
    vmem = pl.BlockSpec(memory_space=pltpu.VMEM)
    smem = pl.BlockSpec(memory_space=pltpu.SMEM)
    dma = pltpu.SemaphoreType.DMA
    return pl.pallas_call(
        kernel,
        out_shape=[jax.ShapeDtypeStruct((ROWS, M // NC), BF)] * 2,
        in_specs=[smem] * 4 + [pl.BlockSpec(memory_space=pl.ANY), vmem, vmem, vmem],
        out_specs=[vmem, vmem],
        scratch_shapes=[
            pltpu.VMEM((NB // 2, ROWS, 2 * BW), BF),
            pltpu.VMEM((NCH, M // SUB, SUB, CW), BF),
            pltpu.VMEM((NCH, ROWS, KT), BF),
            pltpu.VMEM((8, BW, CW), F32),
            pltpu.VMEM((NCH, NR, BW, CW), BF),
            pltpu.VMEM((KT, M // NC), BF),
            pltpu.VMEM((ROWS, M // NC), F32),
            pltpu.VMEM((NR, BW, ROWS), BF),
            pltpu.VMEM((NR, BW, ROWS), BF),
            pltpu.VMEM((NC, 2, BW, ROWS), BF),
            pltpu.VMEM((8, M // NC), F32),
            pltpu.VMEM((8, M // NC), F32),
            pltpu.VMEM((8, M // NC), F32),
            dma((NCH, 3, 7)), dma((NCH, 3, 7)),
            dma((NCH, 8)), dma((NCH, 8)),
            dma((NCH, NR)), dma((NCH, NR)),
            dma((NCH, 3, 7)), dma((NCH, 3, 7)),
            dma((NR,)), dma((NR,)),
            dma((NC,)), dma((NC,)),
            dma((NCH + 2,)),
            dma,
            *[pltpu.VMEM((NR, BW, CW), BF)] * NCH,
        ],
        compiler_params=pltpu.CompilerParams(
            collective_id=0, has_side_effects=True, vmem_limit_bytes=60 << 20
        ),
        cost_estimate=pl.CostEstimate(
            flops=4 * ROWS * M * (M // NC), bytes_accessed=12 << 20, transcendentals=0
        ),
        name="sign_step",
    )(
        inverse * (BW // SUB), inverse // 2, inverse // 8, slot.reshape(-1),
        matrix, position.reshape(1, NB),
        square_pattern, iterate_pattern,
    )


def solution(mesh):
    return jax.shard_map(
        per_device,
        mesh=mesh,
        in_specs=(P("row", None), P(), P(), P()),
        out_specs=(P("row", "col"), P("row", "col")),
        check_vma=False,
    )
```

time: 505 us -> 188 us (0.37)
  waiting for transfers between devices: 409 us -> 0 us
  Pallas kernels: 0 us -> 177 us
  matrix products: 33.4 us -> 0 us
  local copies, waits for them, and re-layouts: 37.2 us -> 5.9 us
  between operations: 13.9 us -> 0.66 us
  starting transfers between devices: 9.6 us -> 0 us
    all_gather x3 -> x0, waiting for transfers between devices: 380 us -> none  [the longest x1 158 us: multiply(): lax.all_gather(own_block, 'col', axis=1, tiled=True)]
    pallas_call x0 -> x1, Pallas kernels: none -> 177 us  [per_device(): pl.pallas_call(kernel, out_shape=[jax.ShapeDtypeStruct((ROWS, M // NC), B...]
    dot_general x4 -> x0, matrix products: 33.4 us -> none  [the longest x2 31.2 us: multiply(): jnp.dot(lax.all_gather(own_block, 'col', axis=1, tiled=True), columns, pr...]
    all_to_all x1 -> x0, waiting for transfers between devices: 28.5 us -> none  [per_device(): lax.all_to_all(outgoing, 'row', split_axis=0, concat_axis=0, tiled=True)]
    mul x4 -> x0, local copies, waits for them, and re-layouts: 11.8 us -> none  [filtered(): values.reshape(row_blocks, BW, col_blocks, BW)]
    all_to_all x1 -> x0, starting transfers between devices: 9.3 us -> none  [per_device(): lax.all_to_all(outgoing, 'row', split_axis=0, concat_axis=0, tiled=True)]
    gather x9 -> x0, local copies, waits for them, and re-layouts: 8.92 us -> none  [the longest x3 6.54 us: per_device(): jnp.take(matrix.reshape(rows_here, blocks, BW), col_atoms, axis=1)]
    unnamed x11 -> x2, local copies, waits for them, and re-layouts: 12 us -> 4.52 us
  transfers between devices with their start and end apart: 4 -> 0, of which waited for: 4 -> 0; matrix products, arithmetic and copies ran while one was open for 3% -> 0% of each run, Pallas kernels for 0% -> 0%
where the time goes in v1:
time: 188 us; the launch traced here: 185 us
  Pallas kernels  177 us (94%)
  local copies, waits for them, and re-layouts  5.9 us (3%)
    pallas_call x1, Pallas kernels, per_device(): pl.pallas_call(kernel, out_shape=[jax.ShapeDtypeStruct((ROWS, M // NC), B...  177 us
    unnamed x2, local copies, waits for them, and re-layouts  4.52 us

profile of v1, /device:TPU:1, one launch (start us, length us, event | category | flops | bytes accessed | tf_op | source)
XLA Modules:
  0.0 184.7 jit_solution(7846080533532406026)
XLA Ops:
  0.6 0.8 select_reduce_fusion.1
  1.4 0.6 and_select_fusion
  1.9 0.7 reshape.73
  2.7 0.1 select_reduce_fusion
  2.8 0.6 reshape.74.slot
  3.5 176.7 %sign_step.1 = (bf16[512,1024]{1,0:T(8,128)(2,1)}, bf16[512,1024]{1,0:T(8,128)(2,1)}) custom-call(s32[128]{0:T(128)} %get-tuple-element.4.first, s32[128]{0:T(128)} %get-tuple-element.3.pair, s32[128]{0:T(128)} %get-tuple-element.2.source, s32[256]{0:T(256)} %reshape.74.slot, bf16[512,8192]{1,0:T(8,128)(2,1)} %m_hbm.1, s32[1,128]{1,0:T(1,128)} %bitcast.1, ...), custom_call_target="tpu_custom_call" | custom-call | flops 17179869184 | bytes 12582912 | tf_op jit(solution)/shard_map/sign_step/pallas_call | solution.py:389
  180.1 2.3 %copy.8 = bf16[512,1024]{1,0:T(8,128)(2,1)} copy(bf16[512,1024]{1,0:T(8,128)(2,1)} %get-tuple-element.7) | data formatting | bytes 2097152
  182.4 2.3 %copy.9 = bf16[512,1024]{1,0:T(8,128)(2,1)} copy(bf16[512,1024]{1,0:T(8,128)(2,1)} %get-tuple-element.8) | data formatting | bytes 2097152
  (1 shorter events, 0.0 us)

commit v2 on v0

v2 whole, which is shorter than its diff:
```python
import jax
import jax.numpy as jnp
from jax import lax
from jax.experimental import pallas as pl
from jax.experimental.pallas import tpu as pltpu
from jax.sharding import PartitionSpec as P

BW = 64
M = 8192
NB = M // BW
ROWS = 512
NR = 16
NC = 8
COLS = M // NC
NCH = 4
CB = NR // NCH
CW = CB * BW
KT = NC * CW
SUB = 16
UNITS = ROWS // SUB
PARTS = ((0, 11), (11, 11), (22, 10))
U = 4
UR = BW // U
MESH = pl.DeviceIdType.MESH
BF = jnp.bfloat16
F32 = jnp.float32


def flip(v, b):
    return v + b - 2 * v * b


def subs(order, o):
    out = [0]
    for d in order[:o]:
        out += [s | (1 << d) for s in out]
    return out


def stage(o):
    for i in range(1 << o):
        for p in range(3):
            order = [(p + n) % 3 for n in range(3)]
            yield p, subs(order, o)[i], order[o]


def kernel(
    first, pair, m_hbm, pos_row, sq_pat, it_pat,
    sq_ref, it_ref,
    mine, mg, fg, facc, mgp, acc, turned, spread, msq, mit, odd, odd_all,
    xs, xr, ds, dr, ns, nr, t1s, t1r, t2s, t2r, loc, m_sem, *got,
):
    r = lax.axis_index("row")
    c = lax.axis_index("col")
    k = r % 2
    y = (r // 2) % 4
    zh = r // 8
    x = c // 2
    zl = c % 2
    jz = flip(zl, zh)
    lab = x * 2 + jz

    def group_col(row):
        return x * 2 + flip(jz, row // 8)

    def outer(mask):
        y_ = y
        if mask & 1:
            y_ = y_ + 1 - 2 * (y_ % 2)
        if mask & 2:
            y_ = 3 - y_
        zh_ = 1 - zh if mask & 4 else zh
        return (zh_ * 4 + y_) * 2 + k

    def inner(mask):
        x_ = x
        if mask & 1:
            x_ = x_ + 1 - 2 * (x_ % 2)
        if mask & 2:
            x_ = 3 - x_
        zl_ = 1 - zl if mask & 4 else zl
        return x_ * 2 + zl_

    def label(col):
        return col // 2 * 2 + flip(col % 2, zh)

    outer_dev = [(outer(1 << d), group_col(outer(1 << d))) for d in range(3)]
    inner_dev = [(r, inner(1 << d)) for d in range(3)]
    sibling = (r + 1 - 2 * k, c)

    def outer_copy(j, p, mask, d, held):
        lo, n = PARTS[p]
        at = mg.at[j, pl.ds(outer(held) * UNITS + lo, n)]
        return pltpu.make_async_remote_copy(
            src_ref=at, dst_ref=at, send_sem=xs.at[j, p, mask - 1], recv_sem=xr.at[j, p, mask - 1],
            device_id=outer_dev[d], device_id_type=MESH,
        )

    def inner_copy(j, p, mask, d, held):
        lo, n = PARTS[p]
        at = fg.at[
            j, pl.ds(lo * SUB, n * SUB), pl.ds(pl.multiple_of(label(inner(held)) * CW, CW), CW)
        ]
        return pltpu.make_async_remote_copy(
            src_ref=at, dst_ref=at, send_sem=ns.at[j, p, mask - 1], recv_sem=nr.at[j, p, mask - 1],
            device_id=inner_dev[d], device_id_type=MESH,
        )

    def sib_copy(j, p, mask, theirs=False):
        lo, n = PARTS[p]
        row = outer(mask)
        if theirs:
            row = row + 1 - 2 * k
        at = mg.at[j, pl.ds(row * UNITS + lo, n)]
        return pltpu.make_async_remote_copy(
            src_ref=at, dst_ref=at, send_sem=ds.at[j, p, mask], recv_sem=dr.at[j, p, mask],
            device_id=sibling, device_id_type=MESH,
        )

    def outer_send(j, o):
        for p, sub, d in stage(o):
            outer_copy(j, p, sub | (1 << d), d, sub).start()

    def outer_wait(j, o):
        for p, sub, d in stage(o):
            mask = sub | (1 << d)
            outer_copy(j, p, mask, d, mask).wait_recv()
            sib_copy(j, p, mask).start()

    def inner_send(j, o):
        for p, sub, d in stage(o):
            inner_copy(j, p, sub | (1 << d), d, sub).start()

    def inner_wait(j, o):
        for p, sub, d in stage(o):
            mask = sub | (1 << d)
            inner_copy(j, p, mask, d, mask).wait_recv()

    def sib_wait(j):
        for mask in range(8):
            for p in range(3):
                sib_copy(j, p, mask, theirs=True).wait_recv()

    def turn1(w, u, t, src_row):
        return pltpu.make_async_remote_copy(
            src_ref=turned.at[w, u, t], dst_ref=got[w * U + u].at[pl.ds(4 * src_row, 4)],
            send_sem=t1s.at[w, u, t], recv_sem=t1r.at[w, u, src_row],
            device_id=(t, group_col(t)), device_id_type=MESH,
        )

    def turn1_own(w, u):
        return pltpu.make_async_copy(
            turned.at[w, u, r], got[w * U + u].at[pl.ds(4 * r, 4)], loc.at[0, w, u]
        )

    def turn2(w, u, col, src_lab):
        out = (sq_ref, it_ref)[w]
        return pltpu.make_async_remote_copy(
            src_ref=spread.at[w, u, col],
            dst_ref=out.at[pl.ds(pl.multiple_of(src_lab * BW + u * UR, UR), UR)],
            send_sem=t2s.at[w, u, col], recv_sem=t2r.at[w, u, src_lab],
            device_id=(r, col), device_id_type=MESH,
        )

    def turn2_own(w, u):
        out = (sq_ref, it_ref)[w]
        return pltpu.make_async_copy(
            spread.at[w, u, c],
            out.at[pl.ds(pl.multiple_of(lab * BW + u * UR, UR), UR)],
            loc.at[1, w, u],
        )

    def turn_store(w, j, values):
        flat = values.T.astype(BF)
        for i in range(CB):
            for u in range(U):
                for n in range(4):
                    lo = i * BW + u * UR
                    turned[w, u, j * CB + i, n] = flat[lo : lo + UR, n * 128 : (n + 1) * 128]

    def turn1_send(w, u):
        for d in range(1, NR):
            turn1(w, u, lax.rem(r + d, NR), r).start()
        turn1_own(w, u).start()

    def turn_on(w, u):
        for d in range(1, NR):
            t = lax.rem(r + NR - d, NR)
            turn1(w, u, t, t).wait_recv()
        turn1_own(w, u).wait()
        have = got[w * U + u]
        lane = lax.broadcasted_iota(jnp.int32, (UR, 128), 1)
        for col in range(NC):
            for g in range(8):
                q = 16 * col + 2 * g
                w0 = have[pair[q]].astype(F32)
                w1 = have[pair[q + 1]].astype(F32)
                o = odd_all[q // 2 : q // 2 + 1, :]
                lo = w0 * (1.0 - o) + pltpu.roll(w0, BW, 1) * o
                hi = w1 * o + pltpu.roll(w1, BW, 1) * (1.0 - o)
                spread[w, u, col, :, g * 128 : (g + 1) * 128] = jnp.where(
                    lane < BW, lo, hi
                ).astype(BF)
        for d in range(1, NC):
            turn2(w, u, lax.rem(c + d, NC), lab).start()
        turn2_own(w, u).start()

    def turn_end(w, u):
        for d in range(1, NC):
            col = lax.rem(c + NC - d, NC)
            turn2(w, u, col, label(col)).wait_recv()
        turn2_own(w, u).wait()

    def columns(j):
        lane = lax.broadcasted_iota(jnp.int32, (ROWS, 2 * BW), 1)
        for i in range(j * CB // 2, (j + 1) * CB // 2):
            w0 = mine[pair[8 * (2 * i) + lab]].astype(F32)
            w1 = mine[pair[8 * (2 * i + 1) + lab]].astype(F32)
            o = odd[0:1, i * 128 : (i + 1) * 128]
            lo = w0 * (1.0 - o) + pltpu.roll(w0, BW, 1) * o
            hi = w1 * o + pltpu.roll(w1, BW, 1) * (1.0 - o)
            both = jnp.where(lane < BW, lo, hi).astype(BF).reshape(UNITS, SUB, 128)
            off = (2 * i) % CB * BW
            mg[j, pl.ds(r * UNITS, UNITS), :, off : off + 128] = both

    def columns_of(rows):
        block_id = lax.broadcasted_iota(jnp.int32, (NR, NB), 0)
        hot = (pos_row[...] == 8 * block_id + lab).astype(F32)
        wide = (
            lax.broadcasted_iota(jnp.int32, (NR, COLS), 1) // BW
            == lax.broadcasted_iota(jnp.int32, (NR, COLS), 0)
        ).astype(F32)
        small = lax.dot_general(rows, hot, (((1,), (1,)), ((), ())), preferred_element_type=F32)
        return jnp.dot(small, wide, preferred_element_type=F32)

    def filters():
        at = pl.ds(pl.multiple_of(8 * r, 8), 8)
        msq[...] = columns_of(sq_pat[at, :].astype(F32))
        mit[...] = columns_of(it_pat[at, :].astype(F32))
        parity = (lax.broadcasted_iota(jnp.int32, (NB, NB), 0) % 2).astype(F32)
        half = lax.broadcasted_iota(jnp.int32, (NB // 2, NB), 0)
        evens = (pos_row[...] == 2 * half).astype(F32)
        odds = (pos_row[...] == 2 * half + 1).astype(F32)
        lane = lax.broadcasted_iota(jnp.int32, (NB // 2, NB), 1)
        odd_all[...] = jnp.where(
            lane < BW,
            jnp.dot(evens, parity, preferred_element_type=F32),
            jnp.dot(odds, parity, preferred_element_type=F32),
        )

    def first_product(j):
        facc[...] = jnp.zeros_like(facc)

        @pl.loop(0, 8)
        def _(kt):
            left = jnp.concatenate([mine[kt * 8 + i] for i in range(8)], axis=1)
            right = mg[j, pl.ds(kt * 64, 64)].reshape(1024, CW)
            facc[...] += jnp.dot(left, right, preferred_element_type=F32)

        at = pl.ds(pl.multiple_of(lab * CW, CW), CW)
        for a in range(8):
            rows = slice(a * BW, (a + 1) * BW)
            value = facc[rows, :] * msq[a : a + 1, j * CW : (j + 1) * CW]
            facc[rows, :] = value
            fg[j, rows, at] = value.astype(BF)

    def second_product(j):
        @pl.loop(0, NC)
        def _(n):
            for i in range(CB):
                src = first[8 * (j * CB + i) + n]
                for u in range(BW // SUB):
                    at = pl.ds(pl.multiple_of(n * CW + i * BW + u * SUB, SUB), SUB)
                    for jj in range(NCH):
                        mgp[at, jj * CW : (jj + 1) * CW] = mg[jj, src + u]

        @pl.loop(0, COLS // 256)
        def _(nt):
            at = pl.ds(pl.multiple_of(nt * 256, 256), 256)
            prod = jnp.dot(fg[j], mgp[:, at], preferred_element_type=F32)
            if j == 0:
                acc[:, at] = prod
            else:
                acc[:, at] += prod

    def iterate_chunk(j):
        own = mg[j, pl.ds(r * UNITS, UNITS)].reshape(ROWS, CW).astype(F32)
        value = 0.5 * (3.0 * own - acc[:, j * CW : (j + 1) * CW])
        for a in range(8):
            rows = slice(a * BW, (a + 1) * BW)
            acc[rows, j * CW : (j + 1) * CW] = (
                value[rows] * mit[a : a + 1, j * CW : (j + 1) * CW]
            )
        turn_store(1, j, acc[:, j * CW : (j + 1) * CW])

    @pl.loop(0, NB // 2)
    def _(i):
        at = pl.ds(pl.multiple_of(i * 128, 128), 128)
        pltpu.make_async_copy(m_hbm.at[:, at], mine.at[i], m_sem).start()

    barrier = pltpu.get_barrier_semaphore()
    for d in range(1, NR):
        t = lax.rem(r + d, NR)
        pl.semaphore_signal(barrier, inc=1, device_id=(t, group_col(t)), device_id_type=MESH)
    for d in range(1, NC):
        pl.semaphore_signal(
            barrier, inc=1, device_id=(r, lax.rem(c + d, NC)), device_id_type=MESH
        )
    odd[...] = columns_of((lax.broadcasted_iota(jnp.int32, (8, NB), 1) % 2).astype(F32))
    pltpu.make_async_copy(mine, mine, m_sem).wait()
    columns(0)
    pl.semaphore_wait(barrier, NR + NC - 2)

    def own_send(j):
        outer_send(j, 0)
        for p in range(3):
            sib_copy(j, p, 0).start()

    own_send(0)
    for j in range(1, NCH):
        columns(j)
    filters()
    for a in range(NCH + 1):
        if a < NCH:
            outer_wait(a, 0)
            outer_send(a, 1)
        if 0 <= a - 2:
            inner_wait(a - 2, 0)
            inner_send(a - 2, 1)
        if a < NCH:
            outer_wait(a, 1)
            outer_send(a, 2)
            if a + 1 < NCH:
                own_send(a + 1)
        if 0 <= a - 2:
            inner_wait(a - 2, 1)
            inner_send(a - 2, 2)
        if 0 <= a - 1:
            outer_wait(a - 1, 2)
            sib_wait(a - 1)
            first_product(a - 1)
            inner_send(a - 1, 0)
            turn_store(0, a - 1, facc[...])

    last = NCH - 1
    for u in range(U):
        turn1_send(0, u)
    for j in range(last):
        inner_wait(j, 2)
    second_product(0)
    inner_wait(last, 0)
    inner_send(last, 1)
    second_product(1)
    inner_wait(last, 1)
    inner_send(last, 2)
    for j in range(2, last):
        second_product(j)
    for u in range(U):
        turn_on(0, u)
    inner_wait(last, 2)
    second_product(last)
    for j in range(NCH):
        iterate_chunk(j)
    for u in range(U):
        turn1_send(1, u)
    for u in range(U):
        turn_on(1, u)
    for w in range(2):
        for u in range(U):
            turn_end(w, u)

    for j in range(NCH):
        for o in range(3):
            for p, sub, d in stage(o):
                outer_copy(j, p, sub | (1 << d), d, sub).wait_send()
                inner_copy(j, p, sub | (1 << d), d, sub).wait_send()
        for p in range(3):
            for mask in range(8):
                sib_copy(j, p, mask).wait_send()
    for w in range(2):
        for u in range(U):
            for d in range(1, NR):
                turn1(w, u, lax.rem(r + d, NR), r).wait_send()
            for d in range(1, NC):
                turn2(w, u, lax.rem(c + d, NC), lab).wait_send()


def per_device(matrix, position, square_pattern, iterate_pattern):
    numbers = jnp.arange(NB, dtype=jnp.int32)
    inverse = jnp.sum(jnp.where(position[:, None] == numbers[None, :], numbers[:, None], 0), axis=0)
    vmem = pl.BlockSpec(memory_space=pltpu.VMEM)
    smem = pl.BlockSpec(memory_space=pltpu.SMEM)
    dma = pltpu.SemaphoreType.DMA
    return pl.pallas_call(
        kernel,
        out_shape=[jax.ShapeDtypeStruct((ROWS, COLS), BF)] * 2,
        in_specs=[smem, smem, pl.BlockSpec(memory_space=pl.ANY), vmem, vmem, vmem],
        out_specs=[vmem, vmem],
        scratch_shapes=[
            pltpu.VMEM((NB // 2, ROWS, 2 * BW), BF),
            pltpu.VMEM((NCH, M // SUB, SUB, CW), BF),
            pltpu.VMEM((NCH, ROWS, KT), BF),
            pltpu.VMEM((ROWS, CW), F32),
            pltpu.VMEM((KT, COLS), BF),
            pltpu.VMEM((ROWS, COLS), F32),
            pltpu.VMEM((2, U, NR, 4, UR, 128), BF),
            pltpu.VMEM((2, U, NC, UR, COLS), BF),
            pltpu.VMEM((8, COLS), F32),
            pltpu.VMEM((8, COLS), F32),
            pltpu.VMEM((8, COLS), F32),
            pltpu.VMEM((NB // 2, 128), F32),
            dma((NCH, 3, 7)), dma((NCH, 3, 7)),
            dma((NCH, 3, 8)), dma((NCH, 3, 8)),
            dma((NCH, 3, 7)), dma((NCH, 3, 7)),
            dma((2, U, NR)), dma((2, U, NR)),
            dma((2, U, NC)), dma((2, U, NC)),
            dma((2, 2, U)),
            dma,
            *[pltpu.VMEM((NB // 2, UR, 128), BF)] * (2 * U),
        ],
        compiler_params=pltpu.CompilerParams(
            collective_id=0, has_side_effects=True, vmem_limit_bytes=60 << 20
        ),
        cost_estimate=pl.CostEstimate(
            flops=4 * ROWS * M * COLS, bytes_accessed=12 << 20, transcendentals=0
        ),
        name="sign_step",
    )(
        inverse * (BW // SUB), inverse // 2, matrix, position.reshape(1, NB),
        square_pattern, iterate_pattern,
    )


def solution(mesh):
    return jax.shard_map(
        per_device,
        mesh=mesh,
        in_specs=(P("row", None), P(), P(), P()),
        out_specs=(P("row", "col"), P("row", "col")),
        check_vma=False,
    )
```

time: 505 us -> 160 us (0.32)
  waiting for transfers between devices: 409 us -> 0 us
  Pallas kernels: 0 us -> 153 us
  matrix products: 33.4 us -> 0 us
  local copies, waits for them, and re-layouts: 37.2 us -> 4.52 us
  between operations: 13.9 us -> 0.64 us
  starting transfers between devices: 9.6 us -> 0 us
    all_gather x3 -> x0, waiting for transfers between devices: 380 us -> none  [the longest x1 158 us: multiply(): lax.all_gather(own_block, 'col', axis=1, tiled=True)]
    pallas_call x0 -> x1, Pallas kernels: none -> 153 us  [per_device(): pl.pallas_call(kernel, out_shape=[jax.ShapeDtypeStruct((ROWS, COLS), BF)]...]
    dot_general x4 -> x0, matrix products: 33.4 us -> none  [the longest x2 31.2 us: multiply(): jnp.dot(lax.all_gather(own_block, 'col', axis=1, tiled=True), columns, pr...]
    all_to_all x1 -> x0, waiting for transfers between devices: 28.5 us -> none  [per_device(): lax.all_to_all(outgoing, 'row', split_axis=0, concat_axis=0, tiled=True)]
    mul x4 -> x0, local copies, waits for them, and re-layouts: 11.8 us -> none  [filtered(): values.reshape(row_blocks, BW, col_blocks, BW)]
    all_to_all x1 -> x0, starting transfers between devices: 9.3 us -> none  [per_device(): lax.all_to_all(outgoing, 'row', split_axis=0, concat_axis=0, tiled=True)]
    gather x9 -> x0, local copies, waits for them, and re-layouts: 8.92 us -> none  [the longest x3 6.54 us: per_device(): jnp.take(matrix.reshape(rows_here, blocks, BW), col_atoms, axis=1)]
    unnamed x11 -> x2, local copies, waits for them, and re-layouts: 12 us -> 4.52 us
  transfers between devices with their start and end apart: 4 -> 0, of which waited for: 4 -> 0; matrix products, arithmetic and copies ran while one was open for 3% -> 0% of each run, Pallas kernels for 0% -> 0%
where the time goes in v2:
time: 160 us
  Pallas kernels  153 us (96%)
  local copies, waits for them, and re-layouts  4.52 us (3%)
    pallas_call x1, Pallas kernels, per_device(): pl.pallas_call(kernel, out_shape=[jax.ShapeDtypeStruct((ROWS, COLS), BF)]...  153 us
    unnamed x2, local copies, waits for them, and re-layouts  4.52 us

profile of v2, /device:TPU:1, one launch (start us, length us, event | category | flops | bytes accessed | tf_op | source)
XLA Modules:
  0.0 159.8 jit_solution(9063092787206375140)
XLA Ops:
  0.6 0.8 select_reduce_fusion
  1.4 0.5 and_select_fusion
  1.9 153.4 %sign_step.1 = (bf16[512,1024]{1,0:T(8,128)(2,1)}, bf16[512,1024]{1,0:T(8,128)(2,1)}) custom-call(s32[128]{0:T(128)} %get-tuple-element.3.first, s32[128]{0:T(128)} %get-tuple-element.2.pair, bf16[512,8192]{1,0:T(8,128)(2,1)} %m_hbm.1, s32[1,128]{1,0:T(1,128)} %bitcast.1, s32[128,128]{1,0:T(8,128)} %sq_pat.1, s32[128,128]{1,0:T(8,128)} %it_pat.1), custom_call_target="tpu_custom_call" | custom-call | flops 17179869184 | bytes 12582912 | tf_op jit(solution)/shard_map/sign_step/pallas_call | solution.py:394
  155.3 2.3 %copy.8 = bf16[512,1024]{1,0:T(8,128)(2,1)} copy(bf16[512,1024]{1,0:T(8,128)(2,1)} %get-tuple-element.6) | data formatting | bytes 2097152
  157.5 2.3 %copy.9 = bf16[512,1024]{1,0:T(8,128)(2,1)} copy(bf16[512,1024]{1,0:T(8,128)(2,1)} %get-tuple-element.7) | data formatting | bytes 2097152

commit v3 on v2

v3 whole, which is shorter than its diff:
```python
import jax
import jax.numpy as jnp
from jax import lax
from jax.experimental import pallas as pl
from jax.experimental.pallas import tpu as pltpu
from jax.sharding import PartitionSpec as P

BW = 64
M = 8192
NB = M // BW
ROWS = 512
NR = 16
NC = 8
COLS = M // NC
TW = 128
NT = COLS // TW
CHUNKS = ((0, 1), (1, 1), (2, 1), (3, 1), (4, 1), (5, 1), (6, 1), (7, 1))
PRODUCTS = ((0, 2), (2, 2), (4, 2), (6, 1), (7, 1))
NCH = len(CHUNKS)
WAVES = ((1, 2, 4), (3, 6, 5), (7,))
SUB = 16
UNITS = ROWS // SUB
PARTS = ((0, 11), (11, 11), (22, 10))
U = 2
UR = BW // U
MESH = pl.DeviceIdType.MESH
OUT, SIB, MUL, IN, TURN, MUL2 = range(6)
ORDER = (
    (OUT, 0, 0), (OUT, 0, 1), (OUT, 1, 0), (SIB, 0, 0), (MUL, 0, 0), (OUT, 1, 1),
    (SIB, 0, 1), (OUT, 2, 0), (SIB, 1, 0), (MUL, 0, 1), (OUT, 0, 2), (SIB, 2, 0),
    (MUL, 1, 0), (OUT, 2, 1), (SIB, 1, 1), (MUL, 2, 0), (IN, 0, 0), (OUT, 0, 3),
    (MUL, 1, 1), (OUT, 1, 2), (SIB, 2, 1), (SIB, 0, 2), (MUL, 2, 1), (IN, 1, 0),
    (IN, 0, 1), (OUT, 1, 3), (SIB, 0, 3), (MUL, 0, 2), (OUT, 2, 2), (SIB, 1, 2),
    (MUL, 0, 3), (OUT, 0, 4), (MUL, 1, 2), (OUT, 2, 3), (SIB, 2, 2), (SIB, 1, 3),
    (IN, 2, 0), (IN, 1, 1), (OUT, 0, 5), (MUL, 2, 2), (IN, 0, 2), (SIB, 2, 3),
    (MUL, 1, 3), (OUT, 1, 4), (SIB, 0, 4), (MUL, 2, 3), (OUT, 1, 5), (IN, 2, 1),
    (IN, 0, 3), (SIB, 0, 5), (MUL, 0, 4), (IN, 1, 2), (OUT, 0, 6), (MUL, 0, 5),
    (OUT, 2, 4), (SIB, 1, 4), (OUT, 2, 5), (SIB, 1, 5), (IN, 1, 3), (MUL, 1, 4),
    (IN, 2, 2), (OUT, 0, 7), (SIB, 2, 4), (MUL, 1, 5), (OUT, 1, 6), (SIB, 2, 5),
    (SIB, 0, 6), (MUL, 2, 4), (IN, 2, 3), (IN, 0, 4), (MUL, 2, 5), (IN, 0, 5),
    (MUL, 0, 6), (OUT, 2, 6), (OUT, 1, 7), (SIB, 1, 6), (SIB, 0, 7), (MUL, 1, 6),
    (IN, 1, 4), (IN, 1, 5), (SIB, 2, 6), (MUL, 0, 7), (OUT, 2, 7), (SIB, 1, 7),
    (MUL, 2, 6), (IN, 0, 6), (MUL, 1, 7), (SIB, 2, 7), (IN, 2, 4), (MUL, 2, 7),
    (IN, 2, 5), (IN, 0, 7), (TURN, 0, 0), (IN, 1, 6), (MUL2, 0, 0), (IN, 1, 7),
    (MUL2, 0, 1), (IN, 2, 6), (MUL2, 0, 2), (IN, 2, 7), (MUL2, 0, 3), (MUL2, 0, 4),
)
BF = jnp.bfloat16
F32 = jnp.float32


def flip(v, b):
    return v + b - 2 * v * b


def message(wave, d):
    held = (0, 1 << (d + 2) % 3, 7 - (1 << d))[wave]
    return held, held | (1 << d)


def kernel(
    first, pair, m_hbm, pos_row, sq_pat, it_pat,
    sq_ref, it_ref,
    mine, mg, fg, facc, acc, turned, spread, msq, mit, odd, odd_all,
    xs, xr, ds, dr, ns, nr, t1s, t1r, t2s, t2r, loc, m_sem, *got,
):
    r = lax.axis_index("row")
    c = lax.axis_index("col")
    k = r % 2
    y = (r // 2) % 4
    zh = r // 8
    x = c // 2
    zl = c % 2
    jz = flip(zl, zh)
    lab = x * 2 + jz

    def group_col(row):
        return x * 2 + flip(jz, row // 8)

    def outer(mask):
        y_ = y
        if mask & 1:
            y_ = y_ + 1 - 2 * (y_ % 2)
        if mask & 2:
            y_ = 3 - y_
        zh_ = 1 - zh if mask & 4 else zh
        return (zh_ * 4 + y_) * 2 + k

    def inner(mask):
        x_ = x
        if mask & 1:
            x_ = x_ + 1 - 2 * (x_ % 2)
        if mask & 2:
            x_ = 3 - x_
        zl_ = 1 - zl if mask & 4 else zl
        return x_ * 2 + zl_

    def label(col):
        return col // 2 * 2 + flip(col % 2, zh)

    outer_dev = [(outer(1 << d), group_col(outer(1 << d))) for d in range(3)]
    inner_dev = [(r, inner(1 << d)) for d in range(3)]
    sibling = (r + 1 - 2 * k, c)

    def outer_copy(j, wave, d, theirs=False):
        lo, n = PARTS[d] if wave == 2 else (0, UNITS)
        at = mg.at[pl.ds(*CHUNKS[j]), pl.ds(outer(message(wave, d)[theirs]) * UNITS + lo, n)]
        return pltpu.make_async_remote_copy(
            src_ref=at, dst_ref=at, send_sem=xs.at[j, wave, d], recv_sem=xr.at[j, wave, d],
            device_id=outer_dev[d], device_id_type=MESH,
        )

    def inner_copy(j, wave, d, theirs=False):
        lo, n = PARTS[d] if wave == 2 else (0, UNITS)
        at = fg.at[
            pl.ds(*CHUNKS[j]), label(inner(message(wave, d)[theirs])), pl.ds(lo * SUB, n * SUB)
        ]
        return pltpu.make_async_remote_copy(
            src_ref=at, dst_ref=at, send_sem=ns.at[j, wave, d], recv_sem=nr.at[j, wave, d],
            device_id=inner_dev[d], device_id_type=MESH,
        )

    def sib_copy(j, mask, theirs=False):
        row = outer(mask)
        if theirs:
            row = row + 1 - 2 * k
        at = mg.at[pl.ds(*CHUNKS[j]), pl.ds(row * UNITS, UNITS)]
        return pltpu.make_async_remote_copy(
            src_ref=at, dst_ref=at, send_sem=ds.at[j, mask], recv_sem=dr.at[j, mask],
            device_id=sibling, device_id_type=MESH,
        )

    def outer_send(j, wave):
        for d in range(3):
            outer_copy(j, wave, d).start()

    def outer_wait(j, wave):
        for d in range(3):
            outer_copy(j, wave, d, theirs=True).wait_recv()

    def sib_send(j, wave):
        for mask in WAVES[wave]:
            sib_copy(j, mask).start()

    def inner_send(j, wave):
        for d in range(3):
            inner_copy(j, wave, d).start()

    def inner_wait(j, wave):
        for d in range(3):
            inner_copy(j, wave, d, theirs=True).wait_recv()

    def sib_wait(j, masks):
        for mask in masks:
            sib_copy(j, mask, theirs=True).wait_recv()

    def turn1(w, u, t, src_row):
        return pltpu.make_async_remote_copy(
            src_ref=turned.at[w, u, t], dst_ref=got[w * U + u].at[pl.ds(4 * src_row, 4)],
            send_sem=t1s.at[w, u, t], recv_sem=t1r.at[w, u, src_row],
            device_id=(t, group_col(t)), device_id_type=MESH,
        )

    def turn1_own(w, u):
        return pltpu.make_async_copy(
            turned.at[w, u, r], got[w * U + u].at[pl.ds(4 * r, 4)], loc.at[0, w, u]
        )

    def turn2(w, u, col, src_lab):
        out = (sq_ref, it_ref)[w]
        return pltpu.make_async_remote_copy(
            src_ref=spread.at[w, u, col],
            dst_ref=out.at[pl.ds(pl.multiple_of(src_lab * BW + u * UR, UR), UR)],
            send_sem=t2s.at[w, u, col], recv_sem=t2r.at[w, u, src_lab],
            device_id=(r, col), device_id_type=MESH,
        )

    def turn2_own(w, u):
        out = (sq_ref, it_ref)[w]
        return pltpu.make_async_copy(
            spread.at[w, u, c],
            out.at[pl.ds(pl.multiple_of(lab * BW + u * UR, UR), UR)],
            loc.at[1, w, u],
        )

    def turn_store(w, tile, tiles, values):
        flat = values.T.astype(BF)
        for i in range(2 * tiles):
            for u in range(U):
                for n in range(4):
                    lo = i * BW + u * UR
                    turned[w, u, 2 * tile + i, n] = flat[lo : lo + UR, n * 128 : (n + 1) * 128]

    def turn1_send(w, u):
        for d in range(1, NR):
            turn1(w, u, lax.rem(r + d, NR), r).start()
        turn1_own(w, u).start()

    def turn_on(w, u):
        for d in range(1, NR):
            t = lax.rem(r + NR - d, NR)
            turn1(w, u, t, t).wait_recv()
        turn1_own(w, u).wait()
        have = got[w * U + u]
        lane = lax.broadcasted_iota(jnp.int32, (UR, 128), 1)
        for col in range(NC):
            for g in range(8):
                q = 16 * col + 2 * g
                w0 = have[pair[q]].astype(F32)
                w1 = have[pair[q + 1]].astype(F32)
                o = odd_all[q // 2 : q // 2 + 1, :]
                lo = w0 * (1.0 - o) + pltpu.roll(w0, BW, 1) * o
                hi = w1 * o + pltpu.roll(w1, BW, 1) * (1.0 - o)
                spread[w, u, col, :, g * 128 : (g + 1) * 128] = jnp.where(
                    lane < BW, lo, hi
                ).astype(BF)
        for d in range(1, NC):
            turn2(w, u, lax.rem(c + d, NC), lab).start()
        turn2_own(w, u).start()

    def turn_end(w, u):
        for d in range(1, NC):
            col = lax.rem(c + NC - d, NC)
            turn2(w, u, col, label(col)).wait_recv()
        turn2_own(w, u).wait()

    def columns(j):
        lane = lax.broadcasted_iota(jnp.int32, (ROWS, TW), 1)
        tile, tiles = CHUNKS[j]
        for i in range(tile, tile + tiles):
            w0 = mine[pair[8 * (2 * i) + lab]].astype(F32)
            w1 = mine[pair[8 * (2 * i + 1) + lab]].astype(F32)
            o = odd[0:1, i * TW : (i + 1) * TW]
            lo = w0 * (1.0 - o) + pltpu.roll(w0, BW, 1) * o
            hi = w1 * o + pltpu.roll(w1, BW, 1) * (1.0 - o)
            both = jnp.where(lane < BW, lo, hi).astype(BF).reshape(UNITS, SUB, TW)
            mg[i, pl.ds(r * UNITS, UNITS)] = both

    def columns_of(rows):
        block_id = lax.broadcasted_iota(jnp.int32, (NR, NB), 0)
        hot = (pos_row[...] == 8 * block_id + lab).astype(F32)
        wide = (
            lax.broadcasted_iota(jnp.int32, (NR, COLS), 1) // BW
            == lax.broadcasted_iota(jnp.int32, (NR, COLS), 0)
        ).astype(F32)
        small = lax.dot_general(rows, hot, (((1,), (1,)), ((), ())), preferred_element_type=F32)
        return jnp.dot(small, wide, preferred_element_type=F32)

    def filters():
        at = pl.ds(pl.multiple_of(8 * r, 8), 8)
        msq[...] = columns_of(sq_pat[at, :].astype(F32))
        mit[...] = columns_of(it_pat[at, :].astype(F32))
        parity = (lax.broadcasted_iota(jnp.int32, (NB, NB), 0) % 2).astype(F32)
        half = lax.broadcasted_iota(jnp.int32, (NB // 2, NB), 0)
        evens = (pos_row[...] == 2 * half).astype(F32)
        odds = (pos_row[...] == 2 * half + 1).astype(F32)
        lane = lax.broadcasted_iota(jnp.int32, (NB // 2, NB), 1)
        odd_all[...] = jnp.where(
            lane < BW,
            jnp.dot(evens, parity, preferred_element_type=F32),
            jnp.dot(odds, parity, preferred_element_type=F32),
        )

    def first_product(j, masks):
        tile, tiles = CHUNKS[j]
        total = facc.at[j % 2, :, 0 : tiles * TW]
        for mask in masks:
            chip = outer(mask) // 2
            left = jnp.concatenate([mine[chip * 8 + i] for i in range(8)], axis=1)
            right = jnp.concatenate(
                [
                    mg[i, pl.ds(chip * 64, 64)].reshape(1024, TW)
                    for i in range(tile, tile + tiles)
                ],
                axis=1,
            )
            prod = jnp.dot(left, right, preferred_element_type=F32)
            if mask == 0:
                total[...] = prod
            else:
                total[...] += prod

    def first_filter(j):
        tile, tiles = CHUNKS[j]
        for a in range(8):
            rows = slice(a * BW, (a + 1) * BW)
            for i in range(tiles):
                at = slice(i * TW, (i + 1) * TW)
                of = slice((tile + i) * TW, (tile + i + 1) * TW)
                value = facc[j % 2, rows, at] * msq[a : a + 1, of]
                facc[j % 2, rows, at] = value
                fg[tile + i, lab, rows, :] = value.astype(BF)

    def second_product(i):
        tile, tiles = PRODUCTS[i]

        @pl.loop(0, COLS // 256)
        def _(nt):
            at = pl.ds(pl.multiple_of(nt * 256, 256), 256)
            left = jnp.concatenate(
                [fg[t, n] for t in range(tile, tile + tiles) for n in range(NC)], axis=1
            )
            right = jnp.concatenate(
                [
                    jnp.concatenate(
                        [mg[nt * 2 + h, first[8 * (2 * t + b) + n] + u] for h in range(2)], axis=1
                    )
                    for t in range(tile, tile + tiles)
                    for n in range(NC)
                    for b in range(2)
                    for u in range(BW // SUB)
                ],
                axis=0,
            )
            prod = jnp.dot(left, right, preferred_element_type=F32)
            if tile == 0:
                acc[:, at] = prod
            else:
                acc[:, at] += prod

    def iterate_tiles(tile):
        own = jnp.concatenate(
            [mg[tile + i, pl.ds(r * UNITS, UNITS)].reshape(ROWS, TW) for i in range(2)], axis=1
        )
        at = slice(tile * TW, (tile + 2) * TW)
        value = 0.5 * (3.0 * own.astype(F32) - acc[:, at])
        kept = [value[a * BW : (a + 1) * BW] * mit[a : a + 1, at] for a in range(8)]
        turn_store(1, tile, 2, jnp.concatenate(kept, axis=0))

    @pl.loop(0, NB // 2)
    def _(i):
        at = pl.ds(pl.multiple_of(i * 128, 128), 128)
        pltpu.make_async_copy(m_hbm.at[:, at], mine.at[i], m_sem).start()

    barrier = pltpu.get_barrier_semaphore()
    for d in range(1, NR):
        t = lax.rem(r + d, NR)
        pl.semaphore_signal(barrier, inc=1, device_id=(t, group_col(t)), device_id_type=MESH)
    for d in range(1, NC):
        pl.semaphore_signal(
            barrier, inc=1, device_id=(r, lax.rem(c + d, NC)), device_id_type=MESH
        )
    odd[...] = columns_of((lax.broadcasted_iota(jnp.int32, (8, NB), 1) % 2).astype(F32))
    pltpu.make_async_copy(mine, mine, m_sem).wait()
    columns(0)
    pl.semaphore_wait(barrier, NR + NC - 2)

    def own_send(j):
        outer_send(j, 0)
        sib_copy(j, 0).start()

    seen = set()

    def once(f, *args):
        if (f, *args) not in seen:
            seen.add((f, *args))
            f(*args)

    for step, wave, j in ORDER:
        if step == OUT:
            if wave == 0:
                once(columns, j)
                own_send(j)
            else:
                once(outer_wait, j, wave - 1)
                outer_send(j, wave)
            if j == 1 and wave == 0:
                for i in range(2, NCH):
                    once(columns, i)
                filters()
        elif step == SIB:
            once(outer_wait, j, wave)
            sib_send(j, wave)
        elif step == MUL:
            masks = ((0, 1, 2, 4), (3, 6, 5), (7,))[wave]
            sib_wait(j, masks)
            first_product(j, masks)
            if wave == 2:
                first_filter(j)
        elif step == IN:
            if wave == 0:
                inner_send(j, 0)
                tile, tiles = CHUNKS[j]
                turn_store(0, tile, tiles, facc[j % 2, :, 0 : tiles * TW])
            else:
                once(inner_wait, j, wave - 1)
                inner_send(j, wave)
        elif step == TURN:
            for u in range(U):
                turn1_send(0, u)
        else:
            for i in range(NCH):
                if CHUNKS[i][0] < sum(PRODUCTS[j]):
                    once(inner_wait, i, 2)
            second_product(j)

    for tile in range(0, NT, 2):
        iterate_tiles(tile)
    for u in range(U):
        turn1_send(1, u)
    for u in range(U):
        turn_on(0, u)
    for u in range(U):
        turn_on(1, u)
    for w in range(2):
        for u in range(U):
            turn_end(w, u)

    for j in range(NCH):
        for wave in range(3):
            for d in range(3):
                outer_copy(j, wave, d).wait_send()
                inner_copy(j, wave, d).wait_send()
        for mask in range(8):
            sib_copy(j, mask).wait_send()
    for w in range(2):
        for u in range(U):
            for d in range(1, NR):
                turn1(w, u, lax.rem(r + d, NR), r).wait_send()
            for d in range(1, NC):
                turn2(w, u, lax.rem(c + d, NC), lab).wait_send()


def per_device(matrix, position, square_pattern, iterate_pattern):
    numbers = jnp.arange(NB, dtype=jnp.int32)
    inverse = jnp.sum(jnp.where(position[:, None] == numbers[None, :], numbers[:, None], 0), axis=0)
    vmem = pl.BlockSpec(memory_space=pltpu.VMEM)
    smem = pl.BlockSpec(memory_space=pltpu.SMEM)
    dma = pltpu.SemaphoreType.DMA
    return pl.pallas_call(
        kernel,
        out_shape=[jax.ShapeDtypeStruct((ROWS, COLS), BF)] * 2,
        in_specs=[smem, smem, pl.BlockSpec(memory_space=pl.ANY), vmem, vmem, vmem],
        out_specs=[vmem, vmem],
        scratch_shapes=[
            pltpu.VMEM((NB // 2, ROWS, 2 * BW), BF),
            pltpu.VMEM((NT, M // SUB, SUB, TW), BF),
            pltpu.VMEM((NT, NC, ROWS, TW), BF),
            pltpu.VMEM((2, ROWS, 2 * TW), F32),
            pltpu.VMEM((ROWS, COLS), F32),
            pltpu.VMEM((2, U, NR, 4, UR, 128), BF),
            pltpu.VMEM((2, U, NC, UR, COLS), BF),
            pltpu.VMEM((8, COLS), F32),
            pltpu.VMEM((8, COLS), F32),
            pltpu.VMEM((8, COLS), F32),
            pltpu.VMEM((NB // 2, 128), F32),
            dma((NCH, 3, 3)), dma((NCH, 3, 3)),
            dma((NCH, NC)), dma((NCH, NC)),
            dma((NCH, 3, 3)), dma((NCH, 3, 3)),
            dma((2, U, NR)), dma((2, U, NR)),
            dma((2, U, NC)), dma((2, U, NC)),
            dma((2, 2, U)),
            dma,
            *[pltpu.VMEM((NB // 2, UR, 128), BF)] * (2 * U),
        ],
        compiler_params=pltpu.CompilerParams(
            collective_id=0, has_side_effects=True, vmem_limit_bytes=60 << 20
        ),
        cost_estimate=pl.CostEstimate(
            flops=4 * ROWS * M * COLS, bytes_accessed=12 << 20, transcendentals=0
        ),
        name="sign_step",
    )(
        inverse * (BW // SUB), inverse // 2, matrix, position.reshape(1, NB),
        square_pattern, iterate_pattern,
    )


def solution(mesh):
    return jax.shard_map(
        per_device,
        mesh=mesh,
        in_specs=(P("row", None), P(), P(), P()),
        out_specs=(P("row", "col"), P("row", "col")),
        check_vma=False,
    )
```

time: 160 us -> 135 us (0.84)
  Pallas kernels: 153 us -> 127 us
    pallas_call x1, Pallas kernels: 153 us -> 127 us  [per_device(): pl.pallas_call(kernel, out_shape=[jax.ShapeDtypeStruct((ROWS, COLS), BF)]...]
where the time goes in v3:
time: 135 us; the launch traced here: 134 us
  Pallas kernels  127 us (94%)
  local copies, waits for them, and re-layouts  4.52 us (3%)
    pallas_call x1, Pallas kernels, per_device(): pl.pallas_call(kernel, out_shape=[jax.ShapeDtypeStruct((ROWS, COLS), BF)]...  127 us
    unnamed x2, local copies, waits for them, and re-layouts  4.52 us

profile of v3, /device:TPU:1, one launch (start us, length us, event | category | flops | bytes accessed | tf_op | source)
XLA Modules:
  0.0 133.6 jit_solution(17792924510899740510)
XLA Ops:
  0.6 0.8 select_reduce_fusion
  1.4 0.5 and_select_fusion
  1.9 127.2 %sign_step.1 = (bf16[512,1024]{1,0:T(8,128)(2,1)}, bf16[512,1024]{1,0:T(8,128)(2,1)}) custom-call(s32[128]{0:T(128)} %get-tuple-element.3.first, s32[128]{0:T(128)} %get-tuple-element.2.pair, bf16[512,8192]{1,0:T(8,128)(2,1)} %m_hbm.1, s32[1,128]{1,0:T(1,128)} %bitcast.1, s32[128,128]{1,0:T(8,128)} %sq_pat.1, s32[128,128]{1,0:T(8,128)} %it_pat.1), custom_call_target="tpu_custom_call" | custom-call | flops 17179869184 | bytes 12582912 | tf_op jit(solution)/shard_map/sign_step/pallas_call | solution.py:429
  129.1 2.3 %copy.8 = bf16[512,1024]{1,0:T(8,128)(2,1)} copy(bf16[512,1024]{1,0:T(8,128)(2,1)} %get-tuple-element.6) | data formatting | bytes 2097152
  131.3 2.3 %copy.9 = bf16[512,1024]{1,0:T(8,128)(2,1)} copy(bf16[512,1024]{1,0:T(8,128)(2,1)} %get-tuple-element.7) | data formatting | bytes 2097152

commit v4 on v3

--- a/solution.py
+++ b/solution.py
@@ -26,22 +26,22 @@
 MESH = pl.DeviceIdType.MESH
 OUT, SIB, MUL, IN, TURN, MUL2 = range(6)
 ORDER = (
-    (OUT, 0, 0), (OUT, 0, 1), (OUT, 1, 0), (SIB, 0, 0), (MUL, 0, 0), (OUT, 1, 1),
-    (SIB, 0, 1), (OUT, 2, 0), (SIB, 1, 0), (MUL, 0, 1), (OUT, 0, 2), (SIB, 2, 0),
-    (MUL, 1, 0), (OUT, 2, 1), (SIB, 1, 1), (MUL, 2, 0), (IN, 0, 0), (OUT, 0, 3),
-    (MUL, 1, 1), (OUT, 1, 2), (SIB, 2, 1), (SIB, 0, 2), (MUL, 2, 1), (IN, 1, 0),
-    (IN, 0, 1), (OUT, 1, 3), (SIB, 0, 3), (MUL, 0, 2), (OUT, 2, 2), (SIB, 1, 2),
-    (MUL, 0, 3), (OUT, 0, 4), (MUL, 1, 2), (OUT, 2, 3), (SIB, 2, 2), (SIB, 1, 3),
-    (IN, 2, 0), (IN, 1, 1), (OUT, 0, 5), (MUL, 2, 2), (IN, 0, 2), (SIB, 2, 3),
-    (MUL, 1, 3), (OUT, 1, 4), (SIB, 0, 4), (MUL, 2, 3), (OUT, 1, 5), (IN, 2, 1),
-    (IN, 0, 3), (SIB, 0, 5), (MUL, 0, 4), (IN, 1, 2), (OUT, 0, 6), (MUL, 0, 5),
-    (OUT, 2, 4), (SIB, 1, 4), (OUT, 2, 5), (SIB, 1, 5), (IN, 1, 3), (MUL, 1, 4),
-    (IN, 2, 2), (OUT, 0, 7), (SIB, 2, 4), (MUL, 1, 5), (OUT, 1, 6), (SIB, 2, 5),
-    (SIB, 0, 6), (MUL, 2, 4), (IN, 2, 3), (IN, 0, 4), (MUL, 2, 5), (IN, 0, 5),
-    (MUL, 0, 6), (OUT, 2, 6), (OUT, 1, 7), (SIB, 1, 6), (SIB, 0, 7), (MUL, 1, 6),
-    (IN, 1, 4), (IN, 1, 5), (SIB, 2, 6), (MUL, 0, 7), (OUT, 2, 7), (SIB, 1, 7),
-    (MUL, 2, 6), (IN, 0, 6), (MUL, 1, 7), (SIB, 2, 7), (IN, 2, 4), (MUL, 2, 7),
-    (IN, 2, 5), (IN, 0, 7), (TURN, 0, 0), (IN, 1, 6), (MUL2, 0, 0), (IN, 1, 7),
+    (OUT, 0, 0), (OUT, 0, 1), (OUT, 1, 0), (SIB, 0, 0), (OUT, 1, 1), (SIB, 0, 1),
+    (MUL, 0, 0), (OUT, 2, 0), (OUT, 0, 2), (SIB, 1, 0), (MUL, 0, 1), (OUT, 2, 1),
+    (SIB, 1, 1), (MUL, 1, 0), (OUT, 0, 3), (SIB, 2, 0), (MUL, 1, 1), (OUT, 1, 2),
+    (SIB, 2, 1), (SIB, 0, 2), (MUL, 2, 0), (IN, 0, 0), (OUT, 0, 4), (OUT, 1, 3),
+    (SIB, 0, 3), (MUL, 2, 1), (IN, 0, 1), (OUT, 2, 2), (SIB, 1, 2), (MUL, 0, 2),
+    (IN, 1, 0), (OUT, 0, 5), (MUL, 1, 2), (IN, 1, 1), (SIB, 2, 2), (MUL, 0, 3),
+    (OUT, 2, 3), (OUT, 1, 4), (SIB, 1, 3), (IN, 2, 0), (SIB, 0, 4), (OUT, 1, 5),
+    (SIB, 0, 5), (MUL, 2, 2), (IN, 2, 1), (IN, 0, 2), (SIB, 2, 3), (MUL, 1, 3),
+    (OUT, 0, 6), (MUL, 0, 4), (OUT, 2, 4), (OUT, 2, 5), (SIB, 1, 4), (SIB, 1, 5),
+    (IN, 1, 2), (OUT, 0, 7), (MUL, 2, 3), (IN, 0, 3), (OUT, 1, 6), (SIB, 0, 6),
+    (SIB, 2, 4), (SIB, 2, 5), (MUL, 1, 4), (MUL, 0, 5), (OUT, 1, 7), (IN, 2, 2),
+    (IN, 1, 3), (SIB, 0, 7), (OUT, 2, 6), (SIB, 1, 6), (MUL, 2, 4), (IN, 0, 4),
+    (MUL, 1, 5), (MUL, 2, 5), (OUT, 2, 7), (IN, 2, 3), (IN, 0, 5), (SIB, 2, 6),
+    (SIB, 1, 7), (MUL, 0, 6), (IN, 1, 4), (SIB, 2, 7), (MUL, 1, 6), (MUL, 2, 6),
+    (IN, 1, 5), (IN, 0, 6), (MUL, 0, 7), (IN, 2, 4), (MUL, 1, 7), (MUL, 2, 7),
+    (IN, 0, 7), (TURN, 0, 0), (IN, 2, 5), (IN, 1, 6), (MUL2, 0, 0), (IN, 1, 7),
     (MUL2, 0, 1), (IN, 2, 6), (MUL2, 0, 2), (IN, 2, 7), (MUL2, 0, 3), (MUL2, 0, 4),
 )
 BF = jnp.bfloat16
@@ -420,13 +420,18 @@
                 turn2(w, u, lax.rem(c + d, NC), lab).wait_send()
 
 
+def hand_over(sq_in, it_in, sq_out, it_out):
+    sq_out[...] = sq_in[...]
+    it_out[...] = it_in[...]
+
+
 def per_device(matrix, position, square_pattern, iterate_pattern):
     numbers = jnp.arange(NB, dtype=jnp.int32)
     inverse = jnp.sum(jnp.where(position[:, None] == numbers[None, :], numbers[:, None], 0), axis=0)
     vmem = pl.BlockSpec(memory_space=pltpu.VMEM)
     smem = pl.BlockSpec(memory_space=pltpu.SMEM)
     dma = pltpu.SemaphoreType.DMA
-    return pl.pallas_call(
+    results = pl.pallas_call(
         kernel,
         out_shape=[jax.ShapeDtypeStruct((ROWS, COLS), BF)] * 2,
         in_specs=[smem, smem, pl.BlockSpec(memory_space=pl.ANY), vmem, vmem, vmem],
@@ -463,6 +468,13 @@
         inverse * (BW // SUB), inverse // 2, matrix, position.reshape(1, NB),
         square_pattern, iterate_pattern,
     )
+    return pl.pallas_call(
+        hand_over,
+        out_shape=[jax.ShapeDtypeStruct((ROWS, COLS), BF)] * 2,
+        in_specs=[vmem, vmem],
+        out_specs=[vmem, vmem],
+        name="hand_over",
+    )(*results)
 
 
 def solution(mesh):

time: 135 us -> 132 us (0.978)
  local copies, waits for them, and re-layouts: 4.52 us -> 0 us
  Pallas kernels: 127 us -> 129 us
    unnamed x2 -> x0, local copies, waits for them, and re-layouts: 4.52 us -> none
    pallas_call x0 -> x1, Pallas kernels: none -> 2.93 us  [per_device(): pl.pallas_call(hand_over, out_shape=[jax.ShapeDtypeStruct((ROWS, COLS), B...]
where the time goes in v4:
time: 132 us; the launch traced here: 131 us
  Pallas kernels  129 us (98%)
    pallas_call x1, Pallas kernels, per_device(): pl.pallas_call(kernel, out_shape=[jax.ShapeDtypeStruct((ROWS, COLS), BF)]...  126 us
    pallas_call x1, Pallas kernels, per_device(): pl.pallas_call(hand_over, out_shape=[jax.ShapeDtypeStruct((ROWS, COLS), B...  2.93 us

profile of v4, /device:TPU:1, one launch (start us, length us, event | category | flops | bytes accessed | tf_op | source)
XLA Modules:
  0.0 131.3 jit_solution(9077467621589489407)
XLA Ops:
  0.6 0.8 select_reduce_fusion
  1.4 0.5 and_select_fusion
  1.9 126.5 %sign_step.1 = (bf16[512,1024]{1,0:T(8,128)(2,1)}, bf16[512,1024]{1,0:T(8,128)(2,1)}) custom-call(s32[128]{0:T(128)} %get-tuple-element.7.first, s32[128]{0:T(128)} %get-tuple-element.6.pair, bf16[512,8192]{1,0:T(8,128)(2,1)} %m_hbm.1, s32[1,128]{1,0:T(1,128)} %bitcast.1, s32[128,128]{1,0:T(8,128)} %sq_pat.1, s32[128,128]{1,0:T(8,128)} %it_pat.1), custom_call_target="tpu_custom_call" | custom-call | flops 17179869184 | bytes 12582912 | tf_op jit(solution)/shard_map/sign_step/pallas_call | solution.py:434
  128.4 2.9 %hand_over.1 = (bf16[512,1024]{1,0:T(8,128)(2,1)}, bf16[512,1024]{1,0:T(8,128)(2,1)}) custom-call(bf16[512,1024]{1,0:T(8,128)(2,1)} %get-tuple-element.4.sq_in, bf16[512,1024]{1,0:T(8,128)(2,1)} %get-tuple-element.5.it_in), custom_call_target="tpu_custom_call" | custom-call | tf_op jit(solution)/shard_map/hand_over/pallas_call | solution.py:471
